TPU v7x, 32 devices: a whole 2x2x4 slice. The times are simulated.
32 devices in a mesh: groups: 2 (over x), store: 16 (over z, y, core).
Axes of the slice: x: 2, y: 2, z: 4, core: 2. Of those that a mesh axis runs over, the one named last changes fastest.
Arguments:
- sources: bfloat16 [16384, 512], P(('groups', 'store')), parts along dimension 0, may hold values from -1800 to 1800
- self_terms: float32 [2, 8192], P(None, 'store'), may hold values from 0.5 to 2
- near_tiles: bfloat16 [2, 32, 5, 256, 256], P(None, 'store'), may hold values from -1 to 1
- near_cols: int32 [32, 5], P('store'), may hold values from 0 to 31, as said below
- near_count: int32 [32], P('store'), may hold values from 1 to 5, as said below
- far_cols: int32 [32, 6], P('store'), may hold values from 0 to 31, as said below
- basis_left: bfloat16 [32, 256, 32], P('store'), may hold values from -2 to 2
- basis_right: bfloat16 [32, 256, 32], P('store'), may hold values from -2 to 2
- couplings: bfloat16 [2, 32, 6, 32, 32], P(None, 'store'), may hold values from -1 to 1
Outputs:
- images: float32 [2, 16384, 512], P(None, ('groups', 'store')), parts along dimension 1
- heights: float32 [4, 512], P('groups'), parts along dimension 0
- norms: float32 [4, 512], P('groups'), parts along dimension 0
There are 2 independent parts, one for each index of `groups`. A program takes and returns all parts, laid end to end along the dimension named above; an argument that names none is the same for every part. Nothing has to cross between parts.
Inputs may be any that keep to these rules, and one draw needn't show every extreme that they name: `near_cols`: the slots of row block i name the blocks i - 2 to i + 2, cyclically, each once, in a drawn order. Slots 0 to near_count - 1 of a row block are live; block 0 has all 5. `far_cols`: a far-field block lies more than 2 blocks from its row block, cyclically.
All inputs are finite; a program needn't handle non-finite values.
Results may differ from a plain program's by a relative error of at most 0.011.
Values may be sent and summed in bfloat16 or wider, within the bound.
A program may use at most 128 MiB of HBM per device.

v0:
```python
import functools

import jax
import jax.numpy as jnp
from jax import lax
from jax.experimental import pallas as pl
from jax.experimental.pallas import tpu as pltpu
from jax.sharding import PartitionSpec as P

REACH = 2
EPSILON = 1e-06
CHUNK = 256
CORES = 2
TINY = 1e-30
MESH = pl.DeviceIdType.MESH
F32 = jnp.float32
BF16 = jnp.bfloat16


def kernel(
    devices,
    cols_ref,
    count_ref,
    far_ref,
    src_ref,
    self_ref,
    tiles_ref,
    left_ref,
    right_ref,
    coup_ref,
    out_ref,
    heights_ref,
    norms_ref,
    w_ref,
    g_ref,
    self_col,
    u1,
    u2,
    z1,
    z2,
    zsel,
    y_ref,
    stats,
    h1_send,
    h1_recv,
    h2_send,
    h2_recv,
    z1_send,
    z1_fsend,
    z1_recv,
    z2_send,
    z2_fsend,
    z2_recv,
    st_send,
    st_recv,
):
    me = lax.axis_index("store")
    chips = devices // CORES
    chip = me // CORES
    core = me % CORES
    partner = chip * CORES + (1 - core)
    right = (me + 1) % devices
    left = (me + devices - 1) % devices
    local = tiles_ref.shape[1]
    near = tiles_ref.shape[2]
    size = tiles_ref.shape[3]
    far = coup_ref.shape[2]
    rank = coup_ref.shape[3]
    rows = local * size
    width = u1.shape[2]
    chunks = u1.shape[0]
    blocks = devices * local
    panels = blocks * size

    def remote(src, dst, send, recv, peer):
        return pltpu.make_async_remote_copy(
            src_ref=src,
            dst_ref=dst,
            send_sem=send,
            recv_sem=recv,
            device_id={"store": peer},
            device_id_type=MESH,
        )

    barrier = pltpu.get_barrier_semaphore()

    @pl.loop(1, devices)
    def _(t):
        pl.semaphore_signal(
            barrier, inc=1, device_id={"store": (me + t) % devices}, device_id_type=MESH
        )

    pl.semaphore_wait(barrier, devices - 1)

    def halo(field, c, send, recv):
        own = field.at[pl.ds(rows, rows)]
        return (
            remote(own, field.at[pl.ds(0, rows)], send.at[c, 0], recv.at[c, 0], right),
            remote(own, field.at[pl.ds(2 * rows, rows)], send.at[c, 1], recv.at[c, 1], left),
        )

    def coeff_copy(z, c, send, recv, source, peer):
        part = z[c].at[pl.ds(source * local, local)]
        return remote(part, part, send, recv.at[c, source], peer)

    def coeff_start(z, c, send, recv):
        coeff_copy(z, c, send.at[c, 0], recv, me, partner).start()

        @pl.loop(1, chips)
        def _(t):
            peer = ((chip + t) % chips) * CORES + core
            coeff_copy(z, c, send.at[c, t], recv, me, peer).start()

    def coeff_forward(z, c, fsend, recv):
        @pl.loop(1, chips)
        def _(t):
            source = ((chip + chips - t) % chips) * CORES + core
            copy = coeff_copy(z, c, fsend.at[c, t], recv, source, partner)
            copy.wait_recv()
            copy.start()

    def coeff_wait(z, c, fsend, recv):
        coeff_copy(z, c, fsend.at[c, 0], recv, partner, partner).wait_recv()

        @pl.loop(1, chips)
        def _(t):
            source = ((chip + chips - t) % chips) * CORES + (1 - core)
            coeff_copy(z, c, fsend.at[c, t], recv, source, partner).wait_recv()

    def coeff_drain(z, c, send, fsend, recv):
        coeff_copy(z, c, send.at[c, 0], recv, me, partner).wait_send()

        @pl.loop(1, chips)
        def _(t):
            coeff_copy(z, c, send.at[c, t], recv, me, partner).wait_send()
            coeff_copy(z, c, fsend.at[c, t], recv, me, partner).wait_send()

    def stat_copy(c, source, peer, t):
        part = stats.at[c, source]
        return remote(part, part, st_send.at[c, t], st_recv.at[c, source], peer)

    def to_coeffs(r, values):
        return jnp.dot(right_ref[r], values, preferred_element_type=F32).astype(BF16)

    for c in range(chunks):
        cut = pl.ds(c * width, width)
        for r in range(local):
            z1[c][me * local + r] = to_coeffs(r, src_ref[pl.ds(r * size, size), cut])
        coeff_start(z1, c, z1_send, z1_recv)
    for c in range(chunks):
        u1[c, pl.ds(rows, rows)] = src_ref[:, pl.ds(c * width, width)]
        for copy in halo(u1.at[c], c, h1_send, h1_recv):
            copy.start()

    for r in range(local):
        row = me * local + r
        for d in range(near):
            target = (row + d - REACH + blocks) % blocks
            slot = jnp.int32(0)
            for k in range(1, near):
                slot = jnp.where(cols_ref[r, k] == target, k, slot)
            live = (slot < count_ref[r]).astype(F32).astype(BF16)
            for o in range(2):
                w_ref[o, r, :, pl.ds(d * size, size)] = tiles_ref[o, r, slot] * live
        for o in range(2):
            parts = [
                lax.dot_general(
                    coup_ref[o, r, k],
                    left_ref[r],
                    (((0,), (0,)), ((), ())),
                    preferred_element_type=F32,
                )
                for k in range(far)
            ]
            parts.append(jnp.zeros((g_ref.shape[3] - far * rank, size), F32))
            g_ref[o, r] = jnp.concatenate(parts, axis=0).T.astype(BF16)
        diag = lax.broadcasted_iota(jnp.int32, (size, size), 0) == lax.broadcasted_iota(
            jnp.int32, (size, size), 1
        )
        for o in range(2):
            line = self_ref[pl.ds(o, 1), pl.ds(r * size, size)]
            self_col[o, pl.ds(r * size, size)] = jnp.sum(
                jnp.where(diag, line, 0.0), axis=1, keepdims=True
            )
    zsel[...] = jnp.zeros_like(zsel)

    def product(o, r, field, z, c, offset):
        for k in range(far):
            zsel[r, pl.ds(k * rank, rank)] = z[c][far_ref[r, k], pl.ds(offset, rank)]
        total = jnp.dot(
            w_ref[o, r],
            field[pl.ds(r * size, near * size)],
            preferred_element_type=F32,
        )
        total += jnp.dot(g_ref[o, r], zsel[r], preferred_element_type=F32)
        own = field[pl.ds(rows + r * size, size)].astype(F32)
        return total + self_col[o, pl.ds(r * size, size)] * own, own

    def first(c):
        coeff_forward(z1, c, z1_fsend, z1_recv)
        coeff_wait(z1, c, z1_fsend, z1_recv)
        for copy in halo(u1.at[c], c, h1_send, h1_recv):
            copy.wait_recv()
        q = jnp.zeros((1, width), F32)
        p = [jnp.zeros((1, width), F32) for _ in range(2)]
        for r in range(local):
            for o in range(2):
                value, own = product(o, r, u1.at[c], z1, c, 0)
                y_ref[c, o, pl.ds(r * size, size)] = value
                p[o] += jnp.sum(value * own, axis=0, keepdims=True)
                if o == 0:
                    q += jnp.sum(own * own, axis=0, keepdims=True)
        h = [p[o] / jnp.maximum(q, TINY) for o in range(2)]
        rest = []
        for o in range(2):
            own = src_ref[:, pl.ds(c * width, width)].astype(F32)
            rem = y_ref[c, o] - h[o] * own
            rest.append(jnp.sum(rem * rem, axis=0, keepdims=True))
        zero = jnp.zeros((1, width), F32)
        stats[c, me] = jnp.concatenate([q, *p, *h, *rest, zero], axis=0)

        @pl.loop(1, devices)
        def _(t):
            stat_copy(c, me, (me + t) % devices, t).start()

    def second(c):
        @pl.loop(1, devices)
        def _(t):
            stat_copy(c, (me + devices - t) % devices, me, t).wait_recv()

        cut = pl.ds(c * width, width)
        every = stats[c]
        sums = jnp.sum(every, axis=0)
        scale = sums[0:1] / panels
        inv = 1.0 / jnp.sqrt(scale + EPSILON)
        own = src_ref[:, cut].astype(F32)
        root = jnp.sqrt(every[:, 0:1])
        for o in range(2):
            h = sums[1 + o : 2 + o] * inv * inv / panels
            off = (every[:, 3 + o : 4 + o] - h[None]) * root
            spread = (sums[5 + o : 6 + o] + jnp.sum(off * off, axis=0)) * inv * inv / panels
            norm = jnp.sqrt(spread + EPSILON)
            heights_ref[pl.ds(o, 1), cut] = h
            norms_ref[pl.ds(o, 1), cut] = norm
            value = ((y_ref[c, o] - h * own) * (inv / norm)).astype(BF16)
            u2[c, o, pl.ds(rows, rows)] = value
            for r in range(local):
                z2[c][me * local + r, pl.ds(o * rank, rank)] = to_coeffs(
                    r, value[r * size : (r + 1) * size]
                )
        coeff_start(z2, c, z2_send, z2_recv)
        for o in range(2):
            for copy in halo(u2.at[c, o], 2 * c + o, h2_send, h2_recv):
                copy.start()

    def third(c):
        coeff_forward(z2, c, z2_fsend, z2_recv)
        coeff_wait(z2, c, z2_fsend, z2_recv)
        for o in range(2):
            for copy in halo(u2.at[c, o], 2 * c + o, h2_send, h2_recv):
                copy.wait_recv()
            for r in range(local):
                value, _ = product(o, r, u2.at[c, o], z2, c, o * rank)
                out_ref[o, pl.ds(r * size, size), pl.ds(c * width, width)] = value

    for c in range(chunks):
        first(c)
        if c >= 1:
            second(c - 1)
    second(chunks - 1)
    for c in range(chunks):
        third(c)

    for c in range(chunks):
        for copy in halo(u1.at[c], c, h1_send, h1_recv):
            copy.wait_send()
        for o in range(2):
            for copy in halo(u2.at[c, o], 2 * c + o, h2_send, h2_recv):
                copy.wait_send()
        coeff_drain(z1, c, z1_send, z1_fsend, z1_recv)
        coeff_drain(z2, c, z2_send, z2_fsend, z2_recv)

        @pl.loop(1, devices)
        def _(t):
            stat_copy(c, me, partner, t).wait_send()


def hand_over(images_ref, heights_ref, norms_ref, out_images, out_heights, out_norms):
    out_images[...] = images_ref[...]
    out_heights[...] = heights_ref[...]
    out_norms[...] = norms_ref[...]


def shards(
    devices,
    sources,
    self_terms,
    near_tiles,
    near_cols,
    near_count,
    far_cols,
    basis_left,
    basis_right,
    couplings,
):
    rows, columns = sources.shape
    local, near, size = near_tiles.shape[1:4]
    far, rank = couplings.shape[2:4]
    blocks = devices * local
    chunks = columns // CHUNK
    chips = devices // CORES
    depth = -(-far * rank // 128) * 128
    dma = pltpu.SemaphoreType.DMA
    smem = pl.BlockSpec(memory_space=pltpu.SMEM)
    vmem = pl.BlockSpec(memory_space=pltpu.VMEM)
    results = pl.pallas_call(
        functools.partial(kernel, devices),
        out_shape=(
            jax.ShapeDtypeStruct((2, rows, columns), F32),
            jax.ShapeDtypeStruct((2, columns), F32),
            jax.ShapeDtypeStruct((2, columns), F32),
        ),
        in_specs=[smem] * 3 + [vmem] * 6,
        out_specs=(vmem,) * 3,
        scratch_shapes=[
            pltpu.VMEM((2, local, size, near * size), BF16),
            pltpu.VMEM((2, local, size, depth), BF16),
            pltpu.VMEM((2, rows, 1), F32),
            pltpu.VMEM((chunks, 3 * rows, CHUNK), BF16),
            pltpu.VMEM((chunks, 2, 3 * rows, CHUNK), BF16),
            [pltpu.VMEM((blocks, rank, CHUNK), BF16)] * chunks,
            [pltpu.VMEM((blocks, 2 * rank, CHUNK), BF16)] * chunks,
            pltpu.VMEM((local, depth, CHUNK), BF16),
            pltpu.VMEM((chunks, 2, rows, CHUNK), F32),
            pltpu.VMEM((chunks, devices, 8, CHUNK), F32),
            dma((chunks, 2)),
            dma((chunks, 2)),
            dma((2 * chunks, 2)),
            dma((2 * chunks, 2)),
            dma((chunks, chips)),
            dma((chunks, chips)),
            dma((chunks, devices)),
            dma((chunks, chips)),
            dma((chunks, chips)),
            dma((chunks, devices)),
            dma((chunks, devices)),
            dma((chunks, devices)),
        ],
        compiler_params=pltpu.CompilerParams(
            collective_id=0, has_side_effects=True, vmem_limit_bytes=56 * 1024 * 1024
        ),
    )(
        near_cols,
        near_count,
        far_cols,
        sources,
        self_terms,
        near_tiles,
        jnp.swapaxes(basis_left, 1, 2),
        jnp.swapaxes(basis_right, 1, 2),
        couplings,
    )
    specs = (
        pl.BlockSpec((1, rows // 2, columns), lambda o, k: (o, k, 0)),
        pl.BlockSpec((2, columns), lambda o, k: (0, 0)),
        pl.BlockSpec((2, columns), lambda o, k: (0, 0)),
    )
    return pl.pallas_call(
        hand_over,
        grid=(2, 2),
        out_shape=tuple(jax.ShapeDtypeStruct(r.shape, r.dtype) for r in results),
        in_specs=specs,
        out_specs=specs,
    )(*results)


def solution(mesh):
    placed = (
        P(("groups", "store"), None),
        P(None, "store"),
        P(None, "store", None, None, None),
        P("store", None),
        P("store"),
        P("store", None),
        P("store", None, None),
        P("store", None, None),
        P(None, "store", None, None, None),
    )
    return jax.shard_map(
        functools.partial(shards, mesh.shape["store"]),
        mesh=mesh,
        in_specs=placed,
        out_specs=(P(None, ("groups", "store"), None), P("groups", None), P("groups", None)),
        check_vma=False,
    )
```

profile of v0, /device:TPU:0, one launch (start us, length us, event | category | flops | bytes accessed | tf_op | source)
XLA Modules:
  0.0 75.5 jit_solution(12334159768541165358)
XLA Ops:
  0.6 71.0 %shard_map.112 = (f32[2,512,512]{2,1,0:T(8,128)}, f32[2,512]{1,0:T(2,128)}, f32[2,512]{1,0:T(2,128)}) custom-call(s32[2,5]{1,0:T(2,128)} %cols_ref.1, s32[2]{0:T(128)} %count_ref.1, s32[2,6]{1,0:T(2,128)} %far_ref.1, bf16[512,512]{1,0:T(8,128)(2,1)} %src_ref.1, f32[2,512]{1,0:T(2,128)} %self_ref.1, bf16[2,2,5,256,256]{4,3,2,1,0:T(8,128)(2,1)} %tiles_ref.1, ...), custom_call_target="tpu_custom_call" | custom-call | tf_op jit(solution)/shard_map/pallas_call | solution.py:316
  71.7 3.8 %shard_map.113 = (f32[2,512,512]{2,1,0:T(8,128)}, f32[2,512]{1,0:T(2,128)}, f32[2,512]{1,0:T(2,128)}) custom-call(f32[2,512,512]{2,1,0:T(8,128)} %get-tuple-element.6.images_ref, f32[2,512]{1,0:T(2,128)} %get-tuple-element.7.heights_ref, f32[2,512]{1,0:T(2,128)} %get-tuple-element.8.norms_ref), custom_call_target="tpu_custom_call" | custom-call | tf_op jit(solution)/shard_map/pallas_call | solution.py:368
where the time goes:
time: 76.2 us; the launch traced here: 75.5 us
  Pallas kernels  74.8 us (98%)
    pallas_call x1, Pallas kernels, shards(): pl.pallas_call(functools.partial(kernel, devices), out_shape=(jax.ShapeDt...  71 us
    pallas_call x1, Pallas kernels, shards(): pl.pallas_call(hand_over, grid=(2, 2), out_shape=tuple((jax.ShapeDtypeStr...  3.8 us

commit v1 on v0

v1 whole, which is shorter than its diff:
```python
import functools

import jax
import jax.numpy as jnp
from jax import lax
from jax.experimental import pallas as pl
from jax.experimental.pallas import tpu as pltpu
from jax.sharding import PartitionSpec as P

REACH = 2
EPSILON = 1e-06
CHUNK = 128
GROUP = 16
RELAY1 = (False, True)
CORES = 2
TINY = 1e-30
MESH = pl.DeviceIdType.MESH
F32 = jnp.float32
BF16 = jnp.bfloat16


def grid_of(devices):
    chips = devices // CORES
    inner = 1
    while inner * inner * 4 <= chips:
        inner *= 2
    return chips // inner, inner


def split3(x):
    high = x.astype(BF16)
    rest = x - high.astype(F32)
    mid = rest.astype(BF16)
    low = (rest - mid.astype(F32)).astype(BF16)
    return [high.astype(F32), mid.astype(F32), low.astype(F32)]


def kernel(
    devices,
    cols_ref,
    count_ref,
    far_ref,
    src_hbm,
    self_hbm,
    tiles_hbm,
    left_hbm,
    right_hbm,
    coup_hbm,
    out_any,
    heights_any,
    norms_any,
    self_ref,
    tiles_ref,
    left_ref,
    right_ref,
    coup_ref,
    out_ref,
    heights_ref,
    norms_ref,
    w_ref,
    g_ref,
    self_col,
    u1,
    u2,
    uw,
    z1,
    z2,
    zsel,
    y_ref,
    in_sem,
    src_sem,
    out_sem,
    h1_send,
    h1_recv,
    h2_send,
    h2_recv,
    y_send,
    y_recv,
    r_send,
    r_recv,
    q_send,
    f_send,
    f_recv,
):
    me = lax.axis_index("store")
    planes, inner = grid_of(devices)
    chips = devices // CORES
    chip = me // CORES
    core = me % CORES
    plane = chip // inner
    place = chip % inner
    half = planes // 2
    partner = chip * CORES + (1 - core)
    right = (me + 1) % devices
    left = (me + devices - 1) % devices
    local, near, size = tiles_ref.shape[1:4]
    far, rank = coup_ref.shape[2:4]
    rows = local * size
    width = u1.shape[2]
    chunks = u1.shape[0]
    blocks = devices * local
    panels = blocks * size
    pieces = rank // GROUP

    def device_at(a, b, k):
        return (a * inner + b) * CORES + k

    def remote(src, dst, send, recv, peer):
        return pltpu.make_async_remote_copy(
            src_ref=src,
            dst_ref=dst,
            send_sem=send,
            recv_sem=recv,
            device_id={"store": peer},
            device_id_type=MESH,
        )

    barrier = pltpu.get_barrier_semaphore()

    def greet(peer):
        pl.semaphore_signal(barrier, inc=1, device_id={"store": peer}, device_id_type=MESH)

    greet(left)
    greet(right)
    for t in range(1, inner):
        greet(device_at(plane, (place + t) % inner, core))
    for t in range(1, planes):
        greet(device_at((plane + t) % planes, place, core))

    def own_copy(c):
        return pltpu.make_async_copy(
            src_hbm.at[:, pl.ds(c * width, width)],
            u1.at[c, pl.ds(rows, rows)],
            src_sem.at[c],
        )

    loads = [
        pltpu.make_async_copy(hbm, vmem, in_sem.at[i])
        for i, (hbm, vmem) in enumerate(
            (
                (right_hbm, right_ref),
                (tiles_hbm, tiles_ref),
                (left_hbm, left_ref),
                (coup_hbm, coup_ref),
                (self_hbm, self_ref),
            )
        )
    ]
    loads[0].start()
    for c in range(chunks):
        own_copy(c).start()
    for load in loads[1:]:
        load.start()

    pl.semaphore_wait(barrier, 2 + inner - 1 + planes - 1)

    def halo1(c):
        own = src_hbm.at[:, pl.ds(c * width, width)]
        return (
            remote(own, u1.at[c, pl.ds(0, rows)], h1_send.at[c, 0], h1_recv.at[c, 0], right),
            remote(own, u1.at[c, pl.ds(2 * rows, rows)], h1_send.at[c, 1], h1_recv.at[c, 1], left),
        )

    def halo2(c, o):
        field = u2.at[c, o]
        own = field.at[pl.ds(rows, rows)]
        return (
            remote(own, field.at[pl.ds(0, rows)], h2_send.at[c, o, 0], h2_recv.at[c, o, 0], right),
            remote(
                own, field.at[pl.ds(2 * rows, rows)], h2_send.at[c, o, 1], h2_recv.at[c, o, 1], left
            ),
        )

    class Gather:
        def __init__(self, z, n, relay):
            self.z, self.n = z, n
            self.relay = relay and planes % 2 == 0 and planes > 2

        def slot(self, k, a, b):
            return self.z.at[k, a, b]

        def row(self, k, a):
            return self.z.at[k, a]

        def across(self, t):
            part = self.slot(core, plane, place)
            peer = device_at(plane, (place + t) % inner, core)
            return remote(part, part, y_send.at[self.n, t], y_recv.at[self.n, t], peer)

        def along(self, t):
            to = (plane + t) % planes
            part = self.row(core, plane)
            return remote(
                part,
                part,
                r_send.at[self.n, t],
                r_recv.at[self.n, plane],
                device_at(to, place, core),
            )

        def goes(self, t):
            if not self.relay:
                return None
            to = (plane + t) % planes
            mine = plane // half
            other = jnp.where(mine == 0, half, half - 1)
            return (to // half == mine) | (to == other)

        def arrival(self, source):
            part = self.row(core, source)
            return remote(part, part, r_send.at[self.n, 0], r_recv.at[self.n, source], partner)

        def passing(self, source, i, t):
            mine = plane // half
            to = mine * half + (plane % half + t) % half
            part = self.row(core, source)
            return remote(
                part,
                part,
                q_send.at[self.n, i, t],
                r_recv.at[self.n, source],
                device_at(to, place, core),
            )

        def is_entry(self):
            return jnp.where(plane < half, half - 1, half) == plane

        def forward(self, source):
            part = self.row(core, source)
            return remote(part, part, f_send.at[self.n, source], f_recv.at[self.n, source], partner)

        def start(self):
            for t in range(1, inner):
                self.across(t).start()

        def rowwise(self):
            for t in range(1, inner):
                self.across(t).wait_recv()
            for t in range(1, planes):
                go = self.goes(t)
                if go is None:
                    self.along(t).start()
                else:
                    pl.when(go)(lambda t=t: self.along(t).start())
            self.forward(plane).start()

        def hand_on(self):
            if not self.relay:
                return
            self.each_pass(True)

        def each_pass(self, starts):
            first = jnp.where(plane < half, half, 0)

            @pl.when(self.is_entry())
            def _():
                for i in range(half):
                    if starts:
                        self.arrival(first + i).wait_recv()
                    for t in range(1, half):
                        copy = self.passing(first + i, i, t)
                        if starts:
                            copy.start()
                        else:
                            copy.wait_send()

        def finish(self):
            for t in range(1, planes):
                source = (plane + t) % planes
                if self.relay:
                    taken = self.is_entry() & (source // half != plane // half)
                    pl.when(jnp.logical_not(taken))(
                        lambda source=source: self.arrival(source).wait_recv()
                    )
                else:
                    self.arrival(source).wait_recv()
                self.forward(source).start()
            for t in range(planes):
                self.forward((plane + t) % planes).wait_recv()

        def drain(self):
            for t in range(1, inner):
                self.across(t).wait_send()
            for t in range(1, planes):
                go = self.goes(t)
                if go is None:
                    self.along(t).wait_send()
                else:
                    pl.when(go)(lambda t=t: self.along(t).wait_send())
            for t in range(planes):
                self.forward((plane + t) % planes).wait_send()
            if self.relay:
                self.each_pass(False)

    gather1 = [Gather(z1[c], c, RELAY1[min(c, len(RELAY1) - 1)]) for c in range(chunks)]
    gather2 = [Gather(z2[c], chunks + c, True) for c in range(chunks)]

    def to_coeffs(r, values):
        return jnp.dot(right_ref[r], values, preferred_element_type=F32).astype(BF16)

    for c in range(chunks):
        for copy in halo1(c):
            copy.start()
    loads[0].wait()
    for c in range(chunks):
        own_copy(c).wait()
        for r in range(local):
            value = to_coeffs(r, u1[c, pl.ds(rows + r * size, size)])
            z1[c][core, plane, place, pl.ds(r * pieces, pieces)] = value.reshape(
                pieces, GROUP, width
            )
        gather1[c].start()
    for load in loads[1:]:
        load.wait()

    def prepare(r):
        row = me * local + r
        for d in range(near):
            target = (row + d - REACH + blocks) % blocks
            slot = jnp.int32(0)
            for k in range(1, near):
                slot = jnp.where(cols_ref[r, k] == target, k, slot)
            live = (slot < count_ref[r]).astype(F32).astype(BF16)
            for o in range(2):
                w_ref[r, pl.ds(o * size, size), pl.ds(d * size, size)] = (
                    tiles_ref[o, r, slot] * live
                )
        for o in range(2):
            parts = [
                lax.dot_general(
                    coup_ref[o, r, k],
                    left_ref[r],
                    (((0,), (0,)), ((), ())),
                    preferred_element_type=F32,
                )
                for k in range(far)
            ]
            if g_ref.shape[2] > far * rank:
                parts.append(jnp.zeros((g_ref.shape[2] - far * rank, size), F32))
            g_ref[r, pl.ds(o * size, size)] = jnp.concatenate(parts, axis=0).T.astype(BF16)
        diag = lax.broadcasted_iota(jnp.int32, (size, size), 0) == lax.broadcasted_iota(
            jnp.int32, (size, size), 1
        )
        for o in range(2):
            line = self_ref[pl.ds(o, 1), pl.ds(r * size, size)]
            self_col[o, pl.ds(r * size, size)] = jnp.sum(
                jnp.where(diag, line, 0.0), axis=1, keepdims=True
            )

    prepare(0)
    for c in range(chunks):
        gather1[c].rowwise()
    for r in range(1, local):
        prepare(r)
    zsel[...] = jnp.zeros_like(zsel)

    def where_is(block):
        owner = block // local
        return owner % CORES, owner // CORES // inner, owner // CORES % inner, block % local

    def first(c):
        for copy in halo1(c):
            copy.wait_recv()
        for r in range(local):
            total = jnp.dot(
                w_ref[r],
                u1[c, pl.ds(r * size, near * size)],
                preferred_element_type=F32,
            )
            for o in range(2):
                y_ref[o, pl.ds(r * size, size)] = total[o * size : (o + 1) * size]
        gather1[c].hand_on()
        gather1[c].finish()
        for r in range(local):
            for k in range(far):
                k_core, a, b, which = where_is(far_ref[r, k])
                zsel[r, pl.ds(k * rank, rank)] = z1[c][
                    k_core, a, b, pl.ds(which * pieces, pieces)
                ].reshape(rank, width)
        q = jnp.zeros((1, width), F32)
        p = [jnp.zeros((1, width), F32) for _ in range(2)]
        for r in range(local):
            more = jnp.dot(g_ref[r], zsel[r], preferred_element_type=F32)
            own = u1[c, pl.ds(rows + r * size, size)].astype(F32)
            q += jnp.sum(own * own, axis=0, keepdims=True)
            for o in range(2):
                at = pl.ds(r * size, size)
                value = y_ref[o, at] + more[o * size : (o + 1) * size] + self_col[o, at] * own
                y_ref[o, at] = value
                p[o] += jnp.sum(value * own, axis=0, keepdims=True)
        h = [p[o] / jnp.maximum(q, TINY) for o in range(2)]
        rest = []
        own = u1[c, pl.ds(rows, rows)].astype(F32)
        for o in range(2):
            rem = y_ref[o] - h[o] * own
            rest.append(jnp.sum(rem * rem, axis=0, keepdims=True))
            value = rem.astype(BF16)
            u2[c, o, pl.ds(rows, rows)] = value
            for r in range(local):
                z2[c][core, plane, place, pl.ds((r * 2 + o) * pieces, pieces)] = to_coeffs(
                    r, value[r * size : (r + 1) * size]
                ).reshape(pieces, GROUP, width)
        lines = []
        for x in (q, *h, *rest):
            lines += split3(x)
        lines.append(jnp.zeros((GROUP - len(lines), width), F32))
        z2[c][core, plane, place, 2 * local * pieces] = jnp.concatenate(lines, axis=0).astype(BF16)
        gather2[c].start()
        for o in range(2):
            for copy in halo2(c, o):
                copy.start()

    def stat(tile, i):
        part = tile[..., 3 * i : 3 * i + 1, :]
        return (
            part
            + tile[..., 3 * i + 1 : 3 * i + 2, :]
            + tile[..., 3 * i + 2 : 3 * i + 3, :]
        )

    def stat_at(c, device):
        k, a, b = device % CORES, device // CORES // inner, device // CORES % inner
        return z2[c][k, a, b, 2 * local * pieces].astype(F32)

    def third(c):
        cut = pl.ds(c * width, width)
        every = z2[c][:, :, :, 2 * local * pieces].astype(F32).reshape(devices, GROUP, width)
        q = stat(every, 0)
        scale = jnp.sum(q, axis=0) / panels
        inv = 1.0 / jnp.sqrt(scale + EPSILON)
        lines = [stat_at(c, left), stat_at(c, me), stat_at(c, right)]
        outs = []
        for o in range(2):
            local_h = stat(every, 1 + o)
            raw = jnp.sum(local_h * q, axis=0)
            h = raw * inv * inv / panels
            off = local_h - h[None]
            spread = jnp.sum(stat(every, 3 + o) + off * off * q, axis=0) * inv * inv / panels
            norm = jnp.sqrt(spread + EPSILON)
            heights_ref[pl.ds(o, 1), cut] = h
            norms_ref[pl.ds(o, 1), cut] = norm
            factor = inv / norm
            for copy in halo2(c, o):
                copy.wait_recv()
            for i, line in enumerate(lines):
                at = pl.ds(i * rows, rows)
                delta = stat(line, 1 + o) - h
                uw[at] = (u2[c, o, at].astype(F32) + delta * u1[c, at].astype(F32)).astype(BF16)
            for r in range(local):
                for k in range(far):
                    k_core, a, b, which = where_is(far_ref[r, k])
                    coeffs = z2[c][
                        k_core, a, b, pl.ds((which * 2 + o) * pieces, pieces)
                    ].reshape(rank, width)
                    base = z1[c][k_core, a, b, pl.ds(which * pieces, pieces)].reshape(rank, width)
                    line = z2[c][k_core, a, b, 2 * local * pieces].astype(F32)
                    delta = stat(line, 1 + o) - h
                    zsel[r, pl.ds(k * rank, rank)] = (
                        coeffs.astype(F32) + delta * base.astype(F32)
                    ).astype(BF16)
                at = pl.ds(r * size, size)
                total = jnp.dot(
                    w_ref[r, pl.ds(o * size, size)],
                    uw[pl.ds(r * size, near * size)],
                    preferred_element_type=F32,
                )
                total += jnp.dot(
                    g_ref[r, pl.ds(o * size, size)], zsel[r], preferred_element_type=F32
                )
                own = uw[pl.ds(rows + r * size, size)].astype(F32)
                out_ref[o, at, cut] = (total + self_col[o, at] * own) * factor
            copy_out(c, o).start()

    def copy_out(c, o):
        cut = pl.ds(c * width, width)
        return pltpu.make_async_copy(out_ref.at[o, :, cut], out_any.at[o, :, cut], out_sem.at[c, o])

    for c in range(chunks):
        first(c)
        if c >= 1:
            gather2[c - 1].rowwise()
        if c >= 2:
            gather2[c - 2].hand_on()
            gather2[c - 2].finish()
    for c in range(max(chunks - 2, 0), chunks):
        if c == chunks - 1:
            gather2[c].rowwise()
        gather2[c].hand_on()
        gather2[c].finish()
    for c in range(chunks):
        third(c)

    small = (
        pltpu.make_async_copy(heights_ref, heights_any, in_sem.at[0]),
        pltpu.make_async_copy(norms_ref, norms_any, in_sem.at[1]),
    )
    for copy in small:
        copy.start()
    for c in range(chunks):
        for copy in halo1(c):
            copy.wait_send()
        for o in range(2):
            for copy in halo2(c, o):
                copy.wait_send()
        gather1[c].drain()
        gather2[c].drain()
    for copy in small:
        copy.wait()
    for c in range(chunks):
        for o in range(2):
            copy_out(c, o).wait()


def hand_over(images_ref, heights_ref, norms_ref, out_images, out_heights, out_norms, sem):
    copies = [
        pltpu.make_async_copy(a, b, sem.at[i])
        for i, (a, b) in enumerate(
            (
                (images_ref, out_images),
                (heights_ref, out_heights),
                (norms_ref, out_norms),
            )
        )
    ]
    for copy in copies:
        copy.start()
    for copy in copies:
        copy.wait()


def shards(
    devices,
    sources,
    self_terms,
    near_tiles,
    near_cols,
    near_count,
    far_cols,
    basis_left,
    basis_right,
    couplings,
):
    rows, columns = sources.shape
    local, near, size = near_tiles.shape[1:4]
    far, rank = couplings.shape[2:4]
    chunks = columns // CHUNK
    planes, inner = grid_of(devices)
    depth = -(-far * rank // 128) * 128
    pieces = rank // GROUP
    dma = pltpu.SemaphoreType.DMA
    smem = pl.BlockSpec(memory_space=pltpu.SMEM)
    hbm = pl.BlockSpec(memory_space=pltpu.HBM)
    anywhere = pl.BlockSpec(memory_space=pl.ANY)
    moved = devices * (3 * local * rank + GROUP) * columns * 2
    gathers = 2 * chunks
    results = pl.pallas_call(
        functools.partial(kernel, devices),
        out_shape=(
            jax.ShapeDtypeStruct((2, rows, columns), F32),
            jax.ShapeDtypeStruct((2, columns), F32),
            jax.ShapeDtypeStruct((2, columns), F32),
        ),
        in_specs=[smem] * 3 + [hbm] * 6,
        out_specs=(anywhere,) * 3,
        scratch_shapes=[
            pltpu.VMEM(self_terms.shape, F32),
            pltpu.VMEM(near_tiles.shape, BF16),
            pltpu.VMEM((local, rank, size), BF16),
            pltpu.VMEM((local, rank, size), BF16),
            pltpu.VMEM(couplings.shape, BF16),
            pltpu.VMEM((2, rows, columns), F32),
            pltpu.VMEM((2, columns), F32),
            pltpu.VMEM((2, columns), F32),
            pltpu.VMEM((local, 2 * size, near * size), BF16),
            pltpu.VMEM((local, 2 * size, depth), BF16),
            pltpu.VMEM((2, rows, 1), F32),
            pltpu.VMEM((chunks, 3 * rows, CHUNK), BF16),
            pltpu.VMEM((chunks, 2, 3 * rows, CHUNK), BF16),
            pltpu.VMEM((3 * rows, CHUNK), BF16),
            [pltpu.VMEM((CORES, planes, inner, local * pieces, GROUP, CHUNK), BF16)] * chunks,
            [pltpu.VMEM((CORES, planes, inner, 2 * local * pieces + 1, GROUP, CHUNK), BF16)]
            * chunks,
            pltpu.VMEM((local, depth, CHUNK), BF16),
            pltpu.VMEM((2, rows, CHUNK), F32),
            dma((5,)),
            dma((chunks,)),
            dma((chunks, 2)),
            dma((chunks, 2)),
            dma((chunks, 2)),
            dma((chunks, 2, 2)),
            dma((chunks, 2, 2)),
            dma((gathers, inner)),
            dma((gathers, inner)),
            dma((gathers, planes)),
            dma((gathers, planes)),
            dma((gathers, max(planes // 2, 1), max(planes // 2, 1))),
            dma((gathers, planes)),
            dma((gathers, planes)),
        ],
        compiler_params=pltpu.CompilerParams(
            collective_id=0, has_side_effects=True, vmem_limit_bytes=24 * 1024 * 1024 + moved
        ),
    )(
        *(
            pltpu.with_memory_space_constraint(x, pltpu.HBM)
            for x in (
                near_cols,
                near_count,
                far_cols,
                sources,
                self_terms,
                near_tiles,
                jnp.swapaxes(basis_left, 1, 2),
                jnp.swapaxes(basis_right, 1, 2),
                couplings,
            )
        )
    )
    return pl.pallas_call(
        hand_over,
        out_shape=tuple(jax.ShapeDtypeStruct(r.shape, r.dtype) for r in results),
        in_specs=(anywhere,) * 3,
        out_specs=(anywhere,) * 3,
        scratch_shapes=[dma((3,))],
        compiler_params=pltpu.CompilerParams(vmem_limit_bytes=1024 * 1024),
    )(*results)


def solution(mesh):
    placed = (
        P(("groups", "store"), None),
        P(None, "store"),
        P(None, "store", None, None, None),
        P("store", None),
        P("store"),
        P("store", None),
        P("store", None, None),
        P("store", None, None),
        P(None, "store", None, None, None),
    )
    return jax.shard_map(
        functools.partial(shards, mesh.shape["store"]),
        mesh=mesh,
        in_specs=placed,
        out_specs=(P(None, ("groups", "store"), None), P("groups", None), P("groups", None)),
        check_vma=False,
    )
```

time: 76.2 us -> 83.7 us (1.098)
  Pallas kernels: 74.8 us -> 81.4 us
    pallas_call x1, Pallas kernels: 71 us -> 80.1 us  [shards(): pl.pallas_call(functools.partial(kernel, devices), out_shape=(jax.ShapeDt...]
    pallas_call x1, Pallas kernels: 3.8 us -> 1.35 us  [shards(): pl.pallas_call(hand_over, out_shape=tuple((jax.ShapeDtypeStruct(r.shape,...]
where the time goes in v1:
time: 83.7 us; the launch traced here: 82.2 us
  Pallas kernels  81.4 us (97%)
    pallas_call x1, Pallas kernels, shards(): pl.pallas_call(functools.partial(kernel, devices), out_shape=(jax.ShapeDt...  80.1 us

profile of v1, /device:TPU:0, one launch (start us, length us, event | category | flops | bytes accessed | tf_op | source)
XLA Modules:
  0.0 82.2 jit_solution(5167783138028975112)
XLA Ops:
  0.6 80.1 %shard_map.112 = (f32[2,512,512]{2,1,0:T(8,128)S(1)}, f32[2,512]{1,0:T(2,128)S(1)}, f32[2,512]{1,0:T(2,128)S(1)}) custom-call(s32[2,5]{1,0:T(2,128)} %cols_ref.1, s32[2]{0:T(128)} %count_ref.1, s32[2,6]{1,0:T(2,128)} %far_ref.1, bf16[512,512]{1,0:T(8,128)(2,1)} %src_hbm.1, f32[2,512]{1,0:T(2,128)} %self_hbm.1, bf16[2,2,5,256,256]{4,3,2,1,0:T(8,128)(2,1)} %tiles_hbm.1, ...), custom_call_target="tpu_custom_call" | custom-call | tf_op jit(solution)/shard_map/pallas_call | solution.py:556
  80.7 1.4 %shard_map.113 = (f32[2,512,512]{2,1,0:T(8,128)}, f32[2,512]{1,0:T(2,128)}, f32[2,512]{1,0:T(2,128)}) custom-call(f32[2,512,512]{2,1,0:T(8,128)S(1)} %get-tuple-element.6.images_ref, f32[2,512]{1,0:T(2,128)S(1)} %get-tuple-element.7.heights_ref, f32[2,512]{1,0:T(2,128)S(1)} %get-tuple-element.8.norms_ref), custom_call_target="tpu_custom_call" | custom-call | tf_op jit(solution)/shard_map/pallas_call | solution.py:619

commit v2 on v1

v2 whole, which is shorter than its diff:
```python
import functools

import jax
import jax.numpy as jnp
from jax import lax
from jax.experimental import pallas as pl
from jax.experimental.pallas import tpu as pltpu
from jax.sharding import PartitionSpec as P

REACH = 2
EPSILON = 1e-06
CHUNK = 128
GROUP = 16
STATS = 3
CORES = 2
TINY = 1e-30
MESH = pl.DeviceIdType.MESH
F32 = jnp.float32
BF16 = jnp.bfloat16


def grid_of(devices):
    chips = devices // CORES
    inner = 1
    while inner * inner * 4 <= chips:
        inner *= 2
    return chips // inner, inner


def chunks_of(columns):
    return columns // CHUNK


def split3(x):
    high = x.astype(BF16)
    rest = x - high.astype(F32)
    mid = rest.astype(BF16)
    low = (rest - mid.astype(F32)).astype(BF16)
    return [high.astype(F32), mid.astype(F32), low.astype(F32)]


def kernel(
    devices,
    cols_ref,
    count_ref,
    far_ref,
    src_hbm,
    self_hbm,
    tiles_hbm,
    left_hbm,
    right_hbm,
    coup_hbm,
    out_any,
    heights_any,
    norms_any,
    self_ref,
    tiles_ref,
    left_ref,
    right_ref,
    coup_ref,
    out_ref,
    heights_ref,
    norms_ref,
    w_ref,
    left_t,
    self_col,
    u1,
    u2,
    uw,
    y_ref,
    zo1,
    zo2,
    zi1,
    zi2,
    zc,
    zsel,
    cm,
    fv,
    fs,
    co1,
    co2,
    ci1,
    ci2,
    in_sem,
    src_sem,
    out_sem,
    fs_sem,
    own_sem,
    h1_send,
    h1_recv,
    h2_send,
    h2_recv,
    m_send,
    m_recv,
    n_send,
    n_recv,
    z_send,
    z_recv,
    y_send,
    y_recv,
    f_send,
    f_recv,
    c_send,
    c_recv,
):
    me = lax.axis_index("store")
    planes, inner = grid_of(devices)
    chips = devices // CORES
    chip = me // CORES
    core = me % CORES
    plane = chip // inner
    place = chip % inner
    homes = planes // chunks_of(src_hbm.shape[1])
    partner = chip * CORES + (1 - core)
    right = (me + 1) % devices
    left = (me + devices - 1) % devices
    local, near, size = tiles_ref.shape[1:4]
    far, rank = coup_ref.shape[2:4]
    rows = local * size
    width = u1.shape[2]
    chunks = u1.shape[0]
    blocks = devices * local
    panels = blocks * size
    pieces = rank // GROUP

    def device_at(a, b, k):
        return (a * inner + b) * CORES + k

    def remote(src, dst, send, recv, peer):
        return pltpu.make_async_remote_copy(
            src_ref=src,
            dst_ref=dst,
            send_sem=send,
            recv_sem=recv,
            device_id={"store": peer},
            device_id_type=MESH,
        )

    barrier = pltpu.get_barrier_semaphore()

    def greet(peer):
        pl.semaphore_signal(barrier, inc=1, device_id={"store": peer}, device_id_type=MESH)

    greet(left)
    greet(right)
    for t in range(1, inner):
        to = (place + t) % inner
        greet(device_at(plane, to, core))
    for t in range(1, planes):
        greet(device_at((plane + t) % planes, place, core))

    def own_copy(c):
        return pltpu.make_async_copy(
            src_hbm.at[:, pl.ds(c * width, width)],
            u1.at[c, pl.ds(rows, rows)],
            src_sem.at[c],
        )

    loads = [
        pltpu.make_async_copy(hbm, vmem, in_sem.at[i])
        for i, (hbm, vmem) in enumerate(
            (
                (right_hbm, right_ref),
                (tiles_hbm, tiles_ref),
                (left_hbm, left_ref),
                (coup_hbm, coup_ref),
                (self_hbm, self_ref),
            )
        )
    ]
    loads[0].start()
    for c in range(chunks):
        own_copy(c).start()
    for load in loads[1:]:
        load.start()

    def halo1(c):
        own = src_hbm.at[:, pl.ds(c * width, width)]
        return (
            remote(own, u1.at[c, pl.ds(0, rows)], h1_send.at[c, 0], h1_recv.at[c, 0], right),
            remote(own, u1.at[c, pl.ds(2 * rows, rows)], h1_send.at[c, 1], h1_recv.at[c, 1], left),
        )

    def halo2(c, o):
        field = u2.at[c, o]
        own = field.at[pl.ds(rows, rows)]
        return (
            remote(own, field.at[pl.ds(0, rows)], h2_send.at[c, o, 0], h2_recv.at[c, o, 0], right),
            remote(
                own, field.at[pl.ds(2 * rows, rows)], h2_send.at[c, o, 1], h2_recv.at[c, o, 1], left
            ),
        )

    def home(c):
        return c * homes

    has_home = plane % homes == 0
    mine = plane // homes
    groups = local * 2 * pieces

    class Stage:
        def __init__(self, n, zo, zi, co, ci):
            self.n, self.zo, self.zi, self.co, self.ci = n, zo, zi, co, ci

        def give_copy(self, c):
            return remote(
                self.zo.at[c],
                self.zi.at[place, core, plane],
                z_send.at[self.n, c],
                z_recv.at[self.n, plane],
                device_at(home(c), place, core),
            )

        def give(self, c):
            @pl.when(plane == home(c))
            def _():
                self.zi[place, core, plane] = self.zo[c]

            @pl.when(plane != home(c))
            def _():
                self.give_copy(c).start()

        def got(self, source):
            part = self.zi.at[place, core, source]
            return remote(part, part, z_send.at[self.n, 0], z_recv.at[self.n, source], partner)

        def across(self, t):
            part = self.zi.at[place, core]
            return remote(
                part,
                part,
                y_send.at[self.n, t],
                y_recv.at[self.n, place],
                device_at(plane, (place + t) % inner, core),
            )

        def crossed(self, source):
            part = self.zi.at[source, core]
            return remote(part, part, y_send.at[self.n, 0], y_recv.at[self.n, source], partner)

        def forward(self, source):
            part = self.zi.at[source, core]
            return remote(part, part, f_send.at[self.n, source], f_recv.at[self.n, source], partner)

        def spread(self):
            @pl.when(has_home)
            def _():
                for t in range(1, planes):
                    self.got((plane + t) % planes).wait_recv()
                for t in range(1, inner):
                    self.across(t).start()
                self.forward(place).start()

        def share(self):
            @pl.when(has_home)
            def _():
                for t in range(1, inner):
                    source = (place + t) % inner
                    self.crossed(source).wait_recv()
                    self.forward(source).start()

        def complete(self):
            @pl.when(has_home)
            def _():
                for b in range(inner):
                    part = self.zi.at[b, 1 - core]
                    remote(
                        part, part, f_send.at[self.n, b], f_recv.at[self.n, b], partner
                    ).wait_recv()

        def back_copy(self, p):
            return remote(
                self.co.at[p],
                self.ci.at[mine],
                c_send.at[self.n, p],
                c_recv.at[self.n, mine],
                device_at(p, place, core),
            )

        def give_back(self):
            @pl.when(has_home)
            def _():
                own = pltpu.make_async_copy(
                    self.co.at[plane], self.ci.at[mine], own_sem.at[self.n]
                )
                own.start()
                for t in range(1, planes):
                    self.back_copy((plane + t) % planes).start()
                own.wait()

        def back(self, c):
            @pl.when(plane != home(c))
            def _():
                part = self.ci.at[c]
                remote(
                    part, part, c_send.at[self.n, 0], c_recv.at[self.n, c], partner
                ).wait_recv()

        def drain(self):
            for c in range(chunks):
                pl.when(plane != home(c))(lambda c=c: self.give_copy(c).wait_send())

            @pl.when(has_home)
            def _():
                for t in range(1, inner):
                    self.across(t).wait_send()
                for b in range(inner):
                    self.forward(b).wait_send()
                for t in range(1, planes):
                    self.back_copy((plane + t) % planes).wait_send()

    stage1 = Stage(0, zo1, zi1, co1, ci1)
    stage2 = Stage(1, zo2, zi2, co2, ci2)

    def to_coeffs(r, values):
        return (
            jnp.dot(right_ref[r], values, preferred_element_type=F32)
            .astype(BF16)
            .reshape(pieces, GROUP, width)
        )

    def table_copies(t):
        to = device_at((plane + t) % planes, place, core)
        m, n = cm.at[plane], fv.at[plane]
        return (
            remote(n, n, n_send.at[t], n_recv.at[plane], to),
            remote(m, m, m_send.at[t], m_recv.at[plane], to),
        )

    def table_waits(t):
        source = (plane + t) % planes
        m, n = cm.at[source], fv.at[source]
        return (
            remote(n, n, n_send.at[t], n_recv.at[source], partner),
            remote(m, m, m_send.at[t], m_recv.at[source], partner),
        )

    def start1(c):
        if c < chunks:
            for copy in halo1(c):
                copy.start()

    loads[0].wait()
    for c in range(chunks):
        own_copy(c).wait()
        for r in range(local):
            value = to_coeffs(r, u1[c, pl.ds(rows + r * size, size)])
            zo1[c, pl.ds(r * pieces, pieces)] = value
    for load in loads[1:]:
        load.wait()
    line = lax.broadcasted_iota(jnp.int32, (8, 128), 0)
    lane = lax.broadcasted_iota(jnp.int32, (8, 128), 1)
    table = jnp.zeros((8, 128), jnp.int32)
    for r in range(local):
        for k in range(far):
            table = jnp.where((line == r) & (lane == k), far_ref[r, k], table)
        for o in range(2):
            parts = [coup_ref[o, r, k] for k in range(far)]
            if cm.shape[3] > far * rank:
                parts.append(jnp.zeros((rank, cm.shape[3] - far * rank), BF16))
            cm[plane, r, pl.ds(o * rank, rank)] = jnp.concatenate(parts, axis=1)
    fv[plane] = table

    pl.semaphore_wait(barrier, 2 + inner - 1 + planes - 1)

    for c in range(chunks):
        stage1.give(c)
    start1(0)
    for t in range(1, planes):
        for copy in table_copies(t):
            copy.start()

    def prepare(r):
        row = me * local + r
        for d in range(near):
            target = (row + d - REACH + blocks) % blocks
            slot = jnp.int32(0)
            for k in range(1, near):
                slot = jnp.where(cols_ref[r, k] == target, k, slot)
            live = (slot < count_ref[r]).astype(F32).astype(BF16)
            for o in range(2):
                w_ref[r, pl.ds(o * size, size), pl.ds(d * size, size)] = (
                    tiles_ref[o, r, slot] * live
                )
        left_t[r] = left_ref[r].astype(F32).T.astype(BF16)
        diag = lax.broadcasted_iota(jnp.int32, (size, size), 0) == lax.broadcasted_iota(
            jnp.int32, (size, size), 1
        )
        for o in range(2):
            line = self_ref[pl.ds(o, 1), pl.ds(r * size, size)]
            self_col[o, pl.ds(r * size, size)] = jnp.sum(
                jnp.where(diag, line, 0.0), axis=1, keepdims=True
            )

    zsel[...] = jnp.zeros_like(zsel)
    prepare(0)

    def where_is(device):
        return device // CORES % inner, device % CORES, device // CORES // inner

    def chosen(z, p, r, k, scale, o):
        block = fs[p, r, k]
        at = (block % local * scale + o) * pieces
        return z[(*where_is(block // local), pl.ds(at, pieces))].reshape(rank, width)

    def sums1():
        @pl.when(has_home)
        def _():
            for p in range(planes):
                for r in range(local):
                    for k in range(far):
                        zsel[0, pl.ds(k * rank, rank)] = chosen(zi1, p, r, k, 1, 0)
                    value = jnp.dot(cm[p, r], zsel[0], preferred_element_type=F32)
                    co1[p, pl.ds(r * 2 * pieces, 2 * pieces)] = value.astype(BF16).reshape(
                        2 * pieces, GROUP, width
                    )

    def stat(tile, i):
        part = tile[..., 3 * i : 3 * i + 1, :]
        return (
            part
            + tile[..., 3 * i + 1 : 3 * i + 2, :]
            + tile[..., 3 * i + 2 : 3 * i + 3, :]
        )

    def sums2():
        @pl.when(has_home)
        def _():
            every = zi2[:, :, :, groups].astype(F32).reshape(devices, GROUP, width)
            q = stat(every, 0)
            scale = jnp.sum(q, axis=0) / panels
            inv = 1.0 / jnp.sqrt(scale + EPSILON)
            totals = []
            for o in range(2):
                local_h = stat(every, 1 + o)
                h = jnp.sum(local_h * q, axis=0) * inv * inv / panels
                off = local_h - h[None]
                spread = jnp.sum(stat(every, 3 + o) + off * off * q, axis=0) * inv * inv / panels
                norm = jnp.sqrt(spread + EPSILON)
                totals.append((inv / norm, h, norm))
                delta = off.reshape(inner, CORES, planes, 1, 1, width)
                for r in range(local):
                    at = pl.ds((r * 2 + o) * pieces, pieces)
                    base = zi1[:, :, :, pl.ds(r * pieces, pieces)].astype(F32)
                    zc[:, :, :, at] = (zi2[:, :, :, at].astype(F32) + delta * base).astype(BF16)
            for p in range(planes):
                for r in range(local):
                    for o in range(2):
                        for k in range(far):
                            zsel[o, pl.ds(k * rank, rank)] = chosen(zc, p, r, k, 2, o)
                        value = jnp.dot(
                            cm[p, r, pl.ds(o * rank, rank)],
                            zsel[o],
                            preferred_element_type=F32,
                        )
                        co2[p, pl.ds((r * 2 + o) * pieces, pieces)] = value.astype(BF16).reshape(
                            pieces, GROUP, width
                        )
                target = device_at(p, place, core)
                lines = []
                for o in range(2):
                    for shift in (devices - 1, 0, 1):
                        tile = zi2[(*where_is((target + shift) % devices), groups)].astype(F32)
                        lines += split3(stat(tile, 1 + o) - totals[o][1])
                    for x in totals[o]:
                        lines += split3(x)
                lines.append(jnp.zeros((STATS * GROUP - len(lines), width), F32))
                co2[p, pl.ds(groups, STATS)] = (
                    jnp.concatenate(lines, axis=0).astype(BF16).reshape(STATS, GROUP, width)
                )

    def first(c):
        for copy in halo1(c):
            copy.wait_recv()
        for r in range(local):
            total = jnp.dot(
                w_ref[r],
                u1[c, pl.ds(r * size, near * size)],
                preferred_element_type=F32,
            )
            for o in range(2):
                y_ref[c, o, pl.ds(r * size, size)] = total[o * size : (o + 1) * size]

    def second(c):
        stage1.back(c)
        q = jnp.zeros((1, width), F32)
        p = [jnp.zeros((1, width), F32) for _ in range(2)]
        for r in range(local):
            own = u1[c, pl.ds(rows + r * size, size)].astype(F32)
            q += jnp.sum(own * own, axis=0, keepdims=True)
            for o in range(2):
                at = pl.ds(r * size, size)
                coeffs = ci1[c, pl.ds((r * 2 + o) * pieces, pieces)].reshape(rank, width)
                more = jnp.dot(left_t[r], coeffs, preferred_element_type=F32)
                value = y_ref[c, o, at] + more + self_col[o, at] * own
                y_ref[c, o, at] = value
                p[o] += jnp.sum(value * own, axis=0, keepdims=True)
        h = [p[o] / jnp.maximum(q, TINY) for o in range(2)]
        rest = []
        own = u1[c, pl.ds(rows, rows)].astype(F32)
        for o in range(2):
            rem = y_ref[c, o] - h[o] * own
            rest.append(jnp.sum(rem * rem, axis=0, keepdims=True))
            value = rem.astype(BF16)
            u2[c, o, pl.ds(rows, rows)] = value
            for r in range(local):
                zo2[c, pl.ds((r * 2 + o) * pieces, pieces)] = to_coeffs(
                    r, value[r * size : (r + 1) * size]
                )
        lines = []
        for x in (q, *h, *rest):
            lines += split3(x)
        lines.append(jnp.zeros((GROUP - len(lines), width), F32))
        zo2[c, groups] = jnp.concatenate(lines, axis=0).astype(BF16)
        stage2.give(c)

    def third(c):
        cut = pl.ds(c * width, width)
        stage2.back(c)
        told = ci2[c, pl.ds(groups, STATS)].astype(F32).reshape(STATS * GROUP, width)
        for o in range(2):
            factor, h, norm = (stat(told, 6 * o + i) for i in range(3, 6))
            heights_ref[pl.ds(o, 1), cut] = h
            norms_ref[pl.ds(o, 1), cut] = norm
            for copy in halo2(c, o):
                copy.wait_recv()
            for i in range(3):
                at = pl.ds(i * rows, rows)
                delta = stat(told, 6 * o + i)
                uw[at] = (u2[c, o, at].astype(F32) + delta * u1[c, at].astype(F32)).astype(BF16)
            for r in range(local):
                at = pl.ds(r * size, size)
                coeffs = ci2[c, pl.ds((r * 2 + o) * pieces, pieces)].reshape(rank, width)
                total = jnp.dot(
                    w_ref[r, pl.ds(o * size, size)],
                    uw[pl.ds(r * size, near * size)],
                    preferred_element_type=F32,
                )
                total += jnp.dot(left_t[r], coeffs, preferred_element_type=F32)
                own = uw[pl.ds(rows + r * size, size)].astype(F32)
                out_ref[o, at, cut] = (total + self_col[o, at] * own) * factor
            copy_out(c, o).start()

    def copy_out(c, o):
        cut = pl.ds(c * width, width)
        return pltpu.make_async_copy(out_ref.at[o, :, cut], out_any.at[o, :, cut], out_sem.at[c, o])

    sent = []

    def send(count):
        for _ in range(count):
            n = len(sent)
            if n < 2 * chunks:
                sent.append(n)
                for copy in halo2(n // 2, n % 2):
                    copy.start()

    stage1.spread()
    start1(1)
    for r in range(1, local):
        prepare(r)
    stage1.share()
    start1(2)
    for t in range(1, planes):
        for copy in table_waits(t):
            copy.wait_recv()
    index = pltpu.make_async_copy(fv, fs, fs_sem)
    index.start()
    stage1.complete()
    index.wait()
    sums1()
    stage1.give_back()
    for c in range(3, chunks):
        start1(c)
    first(0)
    for c in range(chunks):
        second(c)
        if c < 2:
            send(2 - c)
        if c + 1 < chunks:
            first(c + 1)
    stage2.spread()
    send(2)
    stage2.share()
    send(1)
    stage2.complete()
    sums2()
    stage2.give_back()
    send(2 * chunks)
    for c in range(chunks):
        third(c)

    small = (
        pltpu.make_async_copy(heights_ref, heights_any, in_sem.at[0]),
        pltpu.make_async_copy(norms_ref, norms_any, in_sem.at[1]),
    )
    for copy in small:
        copy.start()
    for c in range(chunks):
        for copy in halo1(c):
            copy.wait_send()
        for o in range(2):
            for copy in halo2(c, o):
                copy.wait_send()
    stage1.drain()
    stage2.drain()
    for t in range(1, planes):
        for copy in table_copies(t):
            copy.wait_send()
    for copy in small:
        copy.wait()
    for c in range(chunks):
        for o in range(2):
            copy_out(c, o).wait()


def hand_over(images_ref, heights_ref, norms_ref, out_images, out_heights, out_norms, sem):
    copies = [
        pltpu.make_async_copy(a, b, sem.at[i])
        for i, (a, b) in enumerate(
            (
                (images_ref, out_images),
                (heights_ref, out_heights),
                (norms_ref, out_norms),
            )
        )
    ]
    for copy in copies:
        copy.start()
    for copy in copies:
        copy.wait()


def shards(
    devices,
    sources,
    self_terms,
    near_tiles,
    near_cols,
    near_count,
    far_cols,
    basis_left,
    basis_right,
    couplings,
):
    rows, columns = sources.shape
    local, near, size = near_tiles.shape[1:4]
    far, rank = couplings.shape[2:4]
    chunks = columns // CHUNK
    planes, inner = grid_of(devices)
    depth = -(-far * rank // 128) * 128
    pieces = rank // GROUP
    dma = pltpu.SemaphoreType.DMA
    smem = pl.BlockSpec(memory_space=pltpu.SMEM)
    hbm = pl.BlockSpec(memory_space=pltpu.HBM)
    anywhere = pl.BlockSpec(memory_space=pl.ANY)
    moved = devices * (5 * local * rank + GROUP) * CHUNK * 2
    groups = 2 * local * pieces
    results = pl.pallas_call(
        functools.partial(kernel, devices),
        out_shape=(
            jax.ShapeDtypeStruct((2, rows, columns), F32),
            jax.ShapeDtypeStruct((2, columns), F32),
            jax.ShapeDtypeStruct((2, columns), F32),
        ),
        in_specs=[smem] * 3 + [hbm] * 6,
        out_specs=(anywhere,) * 3,
        scratch_shapes=[
            pltpu.VMEM(self_terms.shape, F32),
            pltpu.VMEM(near_tiles.shape, BF16),
            pltpu.VMEM((local, rank, size), BF16),
            pltpu.VMEM((local, rank, size), BF16),
            pltpu.VMEM(couplings.shape, BF16),
            pltpu.VMEM((2, rows, columns), F32),
            pltpu.VMEM((2, columns), F32),
            pltpu.VMEM((2, columns), F32),
            pltpu.VMEM((local, 2 * size, near * size), BF16),
            pltpu.VMEM((local, size, rank), BF16),
            pltpu.VMEM((2, rows, 1), F32),
            pltpu.VMEM((chunks, 3 * rows, CHUNK), BF16),
            pltpu.VMEM((chunks, 2, 3 * rows, CHUNK), BF16),
            pltpu.VMEM((3 * rows, CHUNK), BF16),
            pltpu.VMEM((chunks, 2, rows, CHUNK), F32),
            pltpu.VMEM((chunks, groups // 2, GROUP, CHUNK), BF16),
            pltpu.VMEM((chunks, groups + 1, GROUP, CHUNK), BF16),
            pltpu.VMEM((inner, CORES, planes, groups // 2, GROUP, CHUNK), BF16),
            pltpu.VMEM((inner, CORES, planes, groups + 1, GROUP, CHUNK), BF16),
            pltpu.VMEM((inner, CORES, planes, groups, GROUP, CHUNK), BF16),
            pltpu.VMEM((2, depth, CHUNK), BF16),
            pltpu.VMEM((planes, local, 2 * rank, depth), BF16),
            pltpu.VMEM((planes, 8, 128), jnp.int32),
            pltpu.SMEM((planes, 8, 128), jnp.int32),
            pltpu.VMEM((planes, groups, GROUP, CHUNK), BF16),
            pltpu.VMEM((planes, groups + STATS, GROUP, CHUNK), BF16),
            pltpu.VMEM((chunks, groups, GROUP, CHUNK), BF16),
            pltpu.VMEM((chunks, groups + STATS, GROUP, CHUNK), BF16),
            dma((5,)),
            dma((chunks,)),
            dma((chunks, 2)),
            dma,
            dma((2,)),
            dma((chunks, 2)),
            dma((chunks, 2)),
            dma((chunks, 2, 2)),
            dma((chunks, 2, 2)),
            dma((planes,)),
            dma((planes,)),
            dma((planes,)),
            dma((planes,)),
            dma((2, chunks)),
            dma((2, planes)),
            dma((2, inner)),
            dma((2, inner)),
            dma((2, inner)),
            dma((2, inner)),
            dma((2, planes)),
            dma((2, chunks)),
        ],
        compiler_params=pltpu.CompilerParams(
            collective_id=0, has_side_effects=True, vmem_limit_bytes=28 * 1024 * 1024 + moved
        ),
    )(
        *(
            pltpu.with_memory_space_constraint(x, pltpu.HBM)
            for x in (
                near_cols,
                near_count,
                far_cols,
                sources,
                self_terms,
                near_tiles,
                jnp.swapaxes(basis_left, 1, 2),
                jnp.swapaxes(basis_right, 1, 2),
                couplings,
            )
        )
    )
    return pl.pallas_call(
        hand_over,
        out_shape=tuple(jax.ShapeDtypeStruct(r.shape, r.dtype) for r in results),
        in_specs=(anywhere,) * 3,
        out_specs=(anywhere,) * 3,
        scratch_shapes=[dma((3,))],
        compiler_params=pltpu.CompilerParams(vmem_limit_bytes=1024 * 1024),
    )(*results)


def solution(mesh):
    placed = (
        P(("groups", "store"), None),
        P(None, "store"),
        P(None, "store", None, None, None),
        P("store", None),
        P("store"),
        P("store", None),
        P("store", None, None),
        P("store", None, None),
        P(None, "store", None, None, None),
    )
    return jax.shard_map(
        functools.partial(shards, mesh.shape["store"]),
        mesh=mesh,
        in_specs=placed,
        out_specs=(P(None, ("groups", "store"), None), P("groups", None), P("groups", None)),
        check_vma=False,
    )
```

time: 83.7 us -> 57 us (0.68); the launches traced: 82.2 us -> 56.9 us
  Pallas kernels: 81.4 us -> 56.2 us
    pallas_call x1, Pallas kernels: 80.1 us -> 54.9 us  [shards(): pl.pallas_call(functools.partial(kernel, devices), out_shape=(jax.ShapeDt...]
where the time goes in v2:
time: 57 us; the launch traced here: 56.9 us
  Pallas kernels  56.2 us (99%)
  between operations  0.64 us (1%)
    pallas_call x1, Pallas kernels, shards(): pl.pallas_call(functools.partial(kernel, devices), out_shape=(jax.ShapeDt...  54.9 us
    pallas_call x1, Pallas kernels, shards(): pl.pallas_call(hand_over, out_shape=tuple((jax.ShapeDtypeStruct(r.shape,...  1.35 us

profile of v2, /device:TPU:0, one launch (start us, length us, event | category | flops | bytes accessed | tf_op | source)
XLA Modules:
  0.0 56.9 jit_solution(4195231819574874202)
XLA Ops:
  0.6 54.9 %shard_map.112 = (f32[2,512,512]{2,1,0:T(8,128)S(1)}, f32[2,512]{1,0:T(2,128)S(1)}, f32[2,512]{1,0:T(2,128)S(1)}) custom-call(s32[2,5]{1,0:T(2,128)} %cols_ref.1, s32[2]{0:T(128)} %count_ref.1, s32[2,6]{1,0:T(2,128)} %far_ref.1, bf16[512,512]{1,0:T(8,128)(2,1)} %src_hbm.1, f32[2,512]{1,0:T(2,128)} %self_hbm.1, bf16[2,2,5,256,256]{4,3,2,1,0:T(8,128)(2,1)} %tiles_hbm.1, ...), custom_call_target="tpu_custom_call" | custom-call | tf_op jit(solution)/shard_map/pallas_call | solution.py:659
  55.5 1.4 %shard_map.113 = (f32[2,512,512]{2,1,0:T(8,128)}, f32[2,512]{1,0:T(2,128)}, f32[2,512]{1,0:T(2,128)}) custom-call(f32[2,512,512]{2,1,0:T(8,128)S(1)} %get-tuple-element.6.images_ref, f32[2,512]{1,0:T(2,128)S(1)} %get-tuple-element.7.heights_ref, f32[2,512]{1,0:T(2,128)S(1)} %get-tuple-element.8.norms_ref), custom_call_target="tpu_custom_call" | custom-call | tf_op jit(solution)/shard_map/pallas_call | solution.py:738

commit v3 on v2

--- a/solution.py
+++ b/solution.py
@@ -12,6 +12,7 @@
 CHUNK = 128
 GROUP = 16
 STATS = 3
+PACE = (2, 1, 0, 0, 2, 2, 0)
 CORES = 2
 TINY = 1e-30
 MESH = pl.DeviceIdType.MESH
@@ -346,6 +347,11 @@
         for r in range(local):
             value = to_coeffs(r, u1[c, pl.ds(rows + r * size, size)])
             zo1[c, pl.ds(r * pieces, pieces)] = value
+    pl.semaphore_wait(barrier, 2 + inner - 1 + planes - 1)
+
+    for c in range(chunks):
+        stage1.give(c)
+    start1(0)
     for load in loads[1:]:
         load.wait()
     line = lax.broadcasted_iota(jnp.int32, (8, 128), 0)
@@ -361,11 +367,6 @@
             cm[plane, r, pl.ds(o * rank, rank)] = jnp.concatenate(parts, axis=1)
     fv[plane] = table
 
-    pl.semaphore_wait(barrier, 2 + inner - 1 + planes - 1)
-
-    for c in range(chunks):
-        stage1.give(c)
-    start1(0)
     for t in range(1, planes):
         for copy in table_copies(t):
             copy.start()
@@ -566,24 +567,26 @@
             copy.wait_recv()
     index = pltpu.make_async_copy(fv, fs, fs_sem)
     index.start()
+    first(0)
     stage1.complete()
     index.wait()
     sums1()
     stage1.give_back()
     for c in range(3, chunks):
         start1(c)
-    first(0)
+    done = (0, 1)
+    first(1)
     for c in range(chunks):
         second(c)
-        if c < 2:
-            send(2 - c)
-        if c + 1 < chunks:
+        send(PACE[min(c, 3)])
+        if c + 1 < chunks and c + 1 not in done:
             first(c + 1)
     stage2.spread()
-    send(2)
+    send(PACE[4])
     stage2.share()
-    send(1)
+    send(PACE[5])
     stage2.complete()
+    send(PACE[6])
     sums2()
     stage2.give_back()
     send(2 * chunks)

time: 57 us -> 55.7 us (0.977)
  Pallas kernels: 56.2 us -> 54.8 us
    pallas_call x1, Pallas kernels: 54.9 us -> 53.5 us  [shards(): pl.pallas_call(functools.partial(kernel, devices), out_shape=(jax.ShapeDt...]
where the time goes in v3:
time: 55.7 us; the launch traced here: 55.5 us
  Pallas kernels  54.8 us (98%)
  between operations  0.64 us (1%)
    pallas_call x1, Pallas kernels, shards(): pl.pallas_call(functools.partial(kernel, devices), out_shape=(jax.ShapeDt...  53.5 us
    pallas_call x1, Pallas kernels, shards(): pl.pallas_call(hand_over, out_shape=tuple((jax.ShapeDtypeStruct(r.shape,...  1.35 us

profile of v3, /device:TPU:0, one launch (start us, length us, event | category | flops | bytes accessed | tf_op | source)
XLA Modules:
  0.0 55.5 jit_solution(15834776950109260554)
XLA Ops:
  0.6 53.5 %shard_map.112 = (f32[2,512,512]{2,1,0:T(8,128)S(1)}, f32[2,512]{1,0:T(2,128)S(1)}, f32[2,512]{1,0:T(2,128)S(1)}) custom-call(s32[2,5]{1,0:T(2,128)} %cols_ref.1, s32[2]{0:T(128)} %count_ref.1, s32[2,6]{1,0:T(2,128)} %far_ref.1, bf16[512,512]{1,0:T(8,128)(2,1)} %src_hbm.1, f32[2,512]{1,0:T(2,128)} %self_hbm.1, bf16[2,2,5,256,256]{4,3,2,1,0:T(8,128)(2,1)} %tiles_hbm.1, ...), custom_call_target="tpu_custom_call" | custom-call | tf_op jit(solution)/shard_map/pallas_call | solution.py:662
  54.1 1.4 %shard_map.113 = (f32[2,512,512]{2,1,0:T(8,128)}, f32[2,512]{1,0:T(2,128)}, f32[2,512]{1,0:T(2,128)}) custom-call(f32[2,512,512]{2,1,0:T(8,128)S(1)} %get-tuple-element.6.images_ref, f32[2,512]{1,0:T(2,128)S(1)} %get-tuple-element.7.heights_ref, f32[2,512]{1,0:T(2,128)S(1)} %get-tuple-element.8.norms_ref), custom_call_target="tpu_custom_call" | custom-call | tf_op jit(solution)/shard_map/pallas_call | solution.py:741

commit v4 on v3

--- a/solution.py
+++ b/solution.py
@@ -225,19 +225,21 @@
             part = self.zi.at[place, core, source]
             return remote(part, part, z_send.at[self.n, 0], z_recv.at[self.n, source], partner)
 
-        def across(self, t):
-            part = self.zi.at[place, core]
+        def across(self, t, a):
+            part = self.zi.at[place, core, a]
             return remote(
                 part,
                 part,
-                y_send.at[self.n, t],
-                y_recv.at[self.n, place],
+                y_send.at[self.n, t, a],
+                y_recv.at[self.n, place, a],
                 device_at(plane, (place + t) % inner, core),
             )
 
-        def crossed(self, source):
-            part = self.zi.at[source, core]
-            return remote(part, part, y_send.at[self.n, 0], y_recv.at[self.n, source], partner)
+        def crossed(self, source, a):
+            part = self.zi.at[source, core, a]
+            return remote(
+                part, part, y_send.at[self.n, 0, a], y_recv.at[self.n, source, a], partner
+            )
 
         def forward(self, source):
             part = self.zi.at[source, core]
@@ -246,10 +248,12 @@
         def spread(self):
             @pl.when(has_home)
             def _():
-                for t in range(1, planes):
-                    self.got((plane + t) % planes).wait_recv()
-                for t in range(1, inner):
-                    self.across(t).start()
+                for i in range(planes):
+                    a = (plane + i) % planes
+                    if i:
+                        self.got(a).wait_recv()
+                    for t in range(1, inner):
+                        self.across(t, a).start()
                 self.forward(place).start()
 
         def share(self):
@@ -257,7 +261,8 @@
             def _():
                 for t in range(1, inner):
                     source = (place + t) % inner
-                    self.crossed(source).wait_recv()
+                    for a in range(planes):
+                        self.crossed(source, a).wait_recv()
                     self.forward(source).start()
 
         def complete(self):
@@ -304,7 +309,8 @@
             @pl.when(has_home)
             def _():
                 for t in range(1, inner):
-                    self.across(t).wait_send()
+                    for a in range(planes):
+                        self.across(t, a).wait_send()
                 for b in range(inner):
                     self.forward(b).wait_send()
                 for t in range(1, planes):
@@ -712,8 +718,8 @@
             dma((planes,)),
             dma((2, chunks)),
             dma((2, planes)),
-            dma((2, inner)),
-            dma((2, inner)),
+            dma((2, inner, planes)),
+            dma((2, inner, planes)),
             dma((2, inner)),
             dma((2, inner)),
             dma((2, planes)),

time: 55.7 us -> 54.5 us (0.978); the launches traced: 55.5 us -> 53.5 us
  Pallas kernels: 54.8 us -> 52.9 us
    pallas_call x1, Pallas kernels: 53.5 us -> 51.6 us  [shards(): pl.pallas_call(functools.partial(kernel, devices), out_shape=(jax.ShapeDt...]
where the time goes in v4:
time: 54.5 us; the launch traced here: 53.5 us
  Pallas kernels  52.9 us (97%)
  between operations  0.64 us (1%)
    pallas_call x1, Pallas kernels, shards(): pl.pallas_call(functools.partial(kernel, devices), out_shape=(jax.ShapeDt...  51.6 us
    pallas_call x1, Pallas kernels, shards(): pl.pallas_call(hand_over, out_shape=tuple((jax.ShapeDtypeStruct(r.shape,...  1.35 us

profile of v4, /device:TPU:0, one launch (start us, length us, event | category | flops | bytes accessed | tf_op | source)
XLA Modules:
  0.0 53.5 jit_solution(12437853999835820662)
XLA Ops:
  0.6 51.6 %shard_map.112 = (f32[2,512,512]{2,1,0:T(8,128)S(1)}, f32[2,512]{1,0:T(2,128)S(1)}, f32[2,512]{1,0:T(2,128)S(1)}) custom-call(s32[2,5]{1,0:T(2,128)} %cols_ref.1, s32[2]{0:T(128)} %count_ref.1, s32[2,6]{1,0:T(2,128)} %far_ref.1, bf16[512,512]{1,0:T(8,128)(2,1)} %src_hbm.1, f32[2,512]{1,0:T(2,128)} %self_hbm.1, bf16[2,2,5,256,256]{4,3,2,1,0:T(8,128)(2,1)} %tiles_hbm.1, ...), custom_call_target="tpu_custom_call" | custom-call | tf_op jit(solution)/shard_map/pallas_call | solution.py:668
  52.2 1.4 %shard_map.113 = (f32[2,512,512]{2,1,0:T(8,128)}, f32[2,512]{1,0:T(2,128)}, f32[2,512]{1,0:T(2,128)}) custom-call(f32[2,512,512]{2,1,0:T(8,128)S(1)} %get-tuple-element.6.images_ref, f32[2,512]{1,0:T(2,128)S(1)} %get-tuple-element.7.heights_ref, f32[2,512]{1,0:T(2,128)S(1)} %get-tuple-element.8.norms_ref), custom_call_target="tpu_custom_call" | custom-call | tf_op jit(solution)/shard_map/pallas_call | solution.py:747
